TPU v7x, 256 devices: a whole 4x4x8 slice. The times are simulated.
256 devices in a mesh: rx: 32 (over z, x_hi, core), tm: 8 (over y, x_lo).
Axes of the slice: x: 4 (x_hi: 2, x_lo: 2; x = x_hi * 2 + x_lo), y: 4, z: 8, core: 2. Of those that a mesh axis runs over, the one named last changes fastest.
Arguments:
- records: float32 [4096, 24576], P('rx', 'tm'), may hold values from -1000 to 1000, as said below
- source_block: int32 [2], replicated, may hold values from 0 to 63
- quality: int32 [4096], P('rx'), may hold values 0 or 1
Outputs:
- stacks: float32 [2, 64, 101, 4096], P(None, 'tm', None, 'rx')
Inputs may be any that keep to these rules, and one draw needn't show every extreme that they name: Noise records with channel and window gains.
All inputs are finite; a program needn't handle non-finite values. No bound on the sum of `quality` on one device may be relied on, other than what follows from the above.
Results may differ from a plain program's by a relative error of at most 0.0039.
Values may be sent and summed in bfloat16 or wider, within the bound.
A program may use at most 192 MiB of HBM per device.

v0:
```python
import math

import jax
import jax.numpy as jnp
from jax import lax
from jax.sharding import PartitionSpec as P

W = 1024
HALF = 50
LAGS = 101
SRC = 64
STEPS = 2


def broadcast(block, axis, owner):
    block = jnp.where(lax.axis_index(axis) == owner, block, jnp.zeros_like(block))
    return lax.psum(block, axis)


def whiten(records, quality):
    receivers = records.shape[0]
    samples = records.reshape(receivers, records.shape[1] // W, W)
    power = jnp.mean(samples * samples, axis=2, keepdims=True)
    return (samples * lax.rsqrt(power + 1e-06) * quality.astype(jnp.float32)[:, None, None]).astype(
        jnp.bfloat16
    )


def broadcast_block(whitened, block):
    per_device = whitened.shape[0]
    first_row = block * SRC
    owner = first_row // per_device
    offset = first_row - owner * per_device
    local_rows = lax.dynamic_slice_in_dim(whitened, offset, SRC, 0)
    return broadcast(local_rows, "rx", owner)


def lag_split():
    fine_shifts = math.isqrt(LAGS - 1) + 1
    coarse_shifts = -(-LAGS // fine_shifts)
    return (fine_shifts, coarse_shifts)


def source_stack(sources, fine_shifts):
    shifted = [
        jnp.pad(sources, ((0, 0), (0, 0), (offset, fine_shifts - offset)))
        for offset in range(fine_shifts)
    ]
    stacked = jnp.stack(shifted, 1)
    return stacked.reshape(sources.shape[0] * fine_shifts, -1)


def receiver_stack(whitened, fine_shifts, coarse_shifts):
    padded = jnp.pad(whitened, ((0, 0), (0, 0), (HALF, coarse_shifts * fine_shifts - HALF)))
    length = whitened.shape[2] + fine_shifts
    shifted = [
        padded[:, :, number * fine_shifts : number * fine_shifts + length]
        for number in range(coarse_shifts)
    ]
    stacked = jnp.stack(shifted, 1)
    return stacked.reshape(whitened.shape[0] * coarse_shifts, -1)


def lag_products(source_rows, receiver_rows, row_count, receivers, fine_shifts, coarse_shifts):
    products = lax.dot_general(
        source_rows, receiver_rows, (((1,), (1,)), ((), ())), preferred_element_type=jnp.float32
    )
    products = products.reshape(row_count, fine_shifts, receivers, coarse_shifts)
    products = jnp.transpose(products, (0, 3, 1, 2)).reshape(
        row_count, coarse_shifts * fine_shifts, receivers
    )
    return products[:, :LAGS, :]


def on_device(records, source_block, quality):
    receivers = records.shape[0]
    windows_here = records.shape[1] // W
    groups = lax.axis_size("tm")
    weight = 1.0 / math.sqrt(W * windows_here * groups)
    whitened = whiten(records, quality)
    fine_shifts, coarse_shifts = lag_split()
    sources = []
    for number in range(STEPS):
        sources.append(broadcast_block(whitened, source_block[number]))
    share_rows = SRC // groups
    receiver_rows = receiver_stack(whitened, fine_shifts, coarse_shifts)
    source_sets = [source_stack(block_rows, fine_shifts) for block_rows in sources]
    results = []
    for source_rows in source_sets:

        def step_term(first_row, row_count, source_rows=source_rows):
            return (
                lag_products(
                    source_rows, receiver_rows, row_count, receivers, fine_shifts, coarse_shifts
                )
                * weight
            )

        results.append(
            lax.psum_scatter(
                step_term(jnp.int32(0), share_rows * lax.axis_size("tm")),
                "tm",
                scatter_dimension=0,
                tiled=True,
            )
        )
    return jnp.stack(results, 0)


def solution(mesh):
    in_specs = (P("rx", "tm"), P(), P("rx"))
    out_specs = P(None, "tm", None, "rx")
    return jax.shard_map(
        on_device, mesh=mesh, in_specs=in_specs, out_specs=out_specs, check_vma=False
    )
```

profile of v0, /device:TPU:1, one launch (start us, length us, event | category | flops | bytes accessed | tf_op | source)
XLA Modules:
  0.0 485.6 jit_solution(4198167202444544092)
XLA Ops:
  6.5 1.3 fusion.16
  9.1 1.9 copy.7
  11.0 0.2 multiply_reduce_fusion
  11.2 0.7 convert_element_type.41
  11.8 0.2 multiply_convert_fusion
  12.0 1.7 dynamic-slice_select_fusion.1
  13.8 1.2 bitcast_dynamic-update-slice_fusion.20
  15.0 1.1 bitcast_dynamic-update-slice_fusion.19
  16.1 1.1 bitcast_dynamic-update-slice_fusion.18
  17.2 1.1 bitcast_dynamic-update-slice_fusion.17
  18.2 1.1 bitcast_dynamic-update-slice_fusion.16
  19.3 1.2 bitcast_dynamic-update-slice_fusion.15
  20.5 1.0 bitcast_dynamic-update-slice_fusion.14
  21.5 1.1 bitcast_dynamic-update-slice_fusion.13
  22.5 1.1 bitcast_dynamic-update-slice_fusion.12
  23.7 1.1 bitcast_dynamic-update-slice_fusion.11
  24.7 266.0 %all-reduce.26.cloned.1.call-done = (bf16[64,3,1024]{0,2,1:T(8,128)(2,1)}, bf16[64,3,1024]{0,2,1:T(8,128)(2,1)}) async-done(((bf16[64,3,1024]{0,2,1:T(8,128)(2,1)}, bf16[64,3,1024]{0,2,1:T(8,128)(2,1)}), (bf16[64,3,1024]{0,2,1:T(8,128)(2,1)}, bf16[64,3,1024]{0,2,1:T(8,128)(2,1)})) %all-reduce.26.cloned.1.call-update) | async-done | bytes 786448 | tf_op jit(solution)/shard_map/psum | solution.py:17
  290.7 1.4 bitcast_dynamic-update-slice_fusion.31
  292.1 1.4 bitcast_dynamic-update-slice_fusion.30
  293.6 1.4 bitcast_dynamic-update-slice_fusion.29
  295.0 1.4 bitcast_dynamic-update-slice_fusion.28
  296.5 1.4 bitcast_dynamic-update-slice_fusion.27
  297.9 1.4 bitcast_dynamic-update-slice_fusion.26
  299.3 0.3 bitcast_dynamic-update-slice_fusion.25
  299.6 0.3 bitcast_dynamic-update-slice_fusion.24
  299.9 0.2 bitcast_dynamic-update-slice_fusion.23
  300.2 0.3 bitcast_dynamic-update-slice_fusion.22
  300.5 0.2 bitcast_dynamic-update-slice_fusion.10
  300.6 0.3 bitcast_dynamic-update-slice_fusion.9
  300.9 0.3 bitcast_dynamic-update-slice_fusion.8
  301.2 0.3 bitcast_dynamic-update-slice_fusion.7
  301.6 0.3 bitcast_dynamic-update-slice_fusion.6
  301.9 0.3 bitcast_dynamic-update-slice_fusion.5
  302.2 0.3 bitcast_dynamic-update-slice_fusion.4
  302.5 0.3 bitcast_dynamic-update-slice_fusion.3
  302.8 0.2 bitcast_dynamic-update-slice_fusion.2
  303.0 0.3 bitcast_dynamic-update-slice_fusion.1
  303.3 0.6 bitcast_dynamic-update-slice_fusion
  303.9 3.4 copy-done.2
  307.3 10.3 %fusion.6 = f32[64,10,11,128]{3,0,1,2:T(8,128)S(1)} fusion(bf16[128,10,3,1035]{0,3,2,1:T(8,128)(2,1)} %bitcast_dynamic-update-slice_fusion.11, bf16[64,11,3,1035]{0,3,2,1:T(8,128)(2,1)S(1)} %get-tuple-element.12), kind=kOutput, calls=%fused_computation.8 | convolution fusion | flops 5595955200 | bytes 15925120 | tf_op jit(solution)/shard_map/dot_general | solution.py:65
  317.6 0.3 copy.9
  317.9 2.1 slice_multiply_fusion.1
  320.1 12.5 %fusion.11 = f32[64,10,11,128]{3,0,1,2:T(8,128)S(1)} fusion(bf16[128,10,3,1035]{0,3,2,1:T(8,128)(2,1)} %bitcast_dynamic-update-slice_fusion.11, bf16[64,11,3,1035]{0,3,2,1:T(8,128)(2,1)} %copy-done.2), kind=kOutput, calls=%fused_computation.9 | convolution fusion | flops 5595955200 | bytes 15925120 | tf_op jit(solution)/shard_map/dot_general | solution.py:65
  332.6 0.3 copy.11
  332.9 2.1 slice_multiply_fusion
  335.0 61.6 %reduce-scatter.3.cloned.1.call-done = f32[8,101,128]{2,0,1:T(8,128)} async-done(((f32[64,101,128]{2,0,1:T(8,128)}), f32[8,101,128]{2,0,1:T(8,128)}) %reduce-scatter.3.cloned.1.call-update) | async-done | bytes 413712 | tf_op jit(solution)/shard_map/reduce_scatter | solution.py:100
  396.5 80.4 %reduce-scatter.5.cloned.1.call-done = f32[8,101,128]{2,0,1:T(8,128)} async-done(((f32[64,101,128]{2,0,1:T(8,128)}), f32[8,101,128]{2,0,1:T(8,128)}) %reduce-scatter.5.cloned.1.call-update) | async-done | bytes 413712 | tf_op jit(solution)/shard_map/reduce_scatter | solution.py:100
  477.0 2.1 pad_maximum_fusion
  (12 shorter events, 0.2 us)
Async XLA Ops:
  6.5 284.2 %all-reduce.26.cloned.1.call-start = ((), (), s32[]{:S(2)}) async-start(), calls=%async_computation.4 | async-start | bytes 3145728 | tf_op jit(solution)/shard_map/psum | solution.py:17
  13.7 382.8 %reduce-scatter.3.cloned.1.call-start = ((), (), s32[]{:S(2)}) async-start(), calls=%async_computation.2 | async-start | bytes 3723264 | tf_op jit(solution)/shard_map/reduce_scatter | solution.py:100
  290.7 8.6 %copy-start.1 = (bf16[64,3,1024]{0,2,1:T(8,128)(2,1)S(1)}, bf16[64,3,1024]{0,2,1:T(8,128)(2,1)}, u32[]{:S(2)}) copy-start(bf16[64,3,1024]{0,2,1:T(8,128)(2,1)} %get-tuple-element.6) | copy-start | bytes 1179652
  290.7 9.7 %copy-start = (bf16[64,3,1024]{0,2,1:T(8,128)(2,1)S(1)}, bf16[64,3,1024]{0,2,1:T(8,128)(2,1)}, u32[]{:S(2)}) copy-start(bf16[64,3,1024]{0,2,1:T(8,128)(2,1)} %get-tuple-element.5) | copy-start | bytes 1179652
  303.9 3.4 copy-start.2
  320.0 156.9 %reduce-scatter.5.cloned.1.call-start = ((), (), s32[]{:S(2)}) async-start(), calls=%async_computation.3 | async-start | bytes 3723264 | tf_op jit(solution)/shard_map/reduce_scatter | solution.py:100
Sparse Core Ops, SparseCore 0:
  13.9 276.8 all-reduce.25
  320.1 76.3 reduce-scatter.2
  399.3 77.6 reduce-scatter.4
where the time goes:
time: 486 us
  waiting for transfers between devices  408 us (84%)
  local copies, waits for them, and re-layouts  31.1 us (6%)
  matrix products  22.9 us (5%)
  between operations  14.5 us (3%)
  other arithmetic  8.97 us (2%)
    psum x1, waiting for transfers between devices, broadcast(): return lax.psum(block, axis)  266 us
    reduce_scatter x2, waiting for transfers between devices, on_device(): lax.psum_scatter(step_term(jnp.int32(0), share_rows * lax.axis_size('tm')...  142 us
    unnamed x36, local copies, waits for them, and re-layouts  27.6 us
    dot_general x2, matrix products, lag_products(): lax.dot_general(source_rows, receiver_rows, (((1,), (1,)), ((), ())), pre...  22.9 us
  transfers between devices with their start and end apart: 3, of which 3 were waited for; matrix products, arithmetic and copies ran while one was open for 5% of the time, Pallas kernels for 0%

commit v1 on v0

v1 whole, which is shorter than its diff:
```python
import math

import jax
import jax.numpy as jnp
from jax import lax
from jax.experimental import pallas as pl
from jax.experimental.pallas import tpu as pltpu
from jax.sharding import PartitionSpec as P

W = 1024
LAGS = 101
FINE = 8
COARSE = 13
PAD = 48
NZ = 8
NY = 4
WIN = 3
ROWS = W + 2 * PAD
SHARE = WIN * W
PIECE = SHARE // NZ
PAIRS = (COARSE + 1) // 2
WEIGHT = 1.0 / math.sqrt(24 * W)
MESH = pl.DeviceIdType.MESH
F32 = jnp.float32
BF16 = jnp.bfloat16


def device(z, xh, c, y, xl):
    return ((z * 2 + xh) * 2 + c, y * 2 + xl)


def shifted_rows(values, shift):
    return pltpu.roll(values, shift % values.shape[1], 1)


def fill_second_lane_half(ab, w, columns):
    zeros = jnp.zeros((8, 128), F32)
    ab[w, PAD - 16 : PAD + W, 128:256] = jnp.concatenate([zeros, columns, zeros], 0).astype(BF16)


def edge_rows(block, keep_low):
    blocks = block.reshape(PAD // 8, 8, 128)
    rolled = pltpu.roll(blocks, 2, 1)
    row = lax.broadcasted_iota(jnp.int32, rolled.shape, 1)
    keep = row < 2 if keep_low else row >= 2
    return jnp.where(keep, rolled, 0.0)


def fill_edges(re32, w, head, tail):
    low = edge_rows(head, True)
    high = edge_rows(tail, False)
    at = pl.ds(pl.multiple_of(w * 8, 8), 8)
    for m in range(1, PAD // 8 + 1):
        c = 6 + m
        re32[c // 2, at, (c % 2) * 128 : (c % 2) * 128 + 128] = low[m - 1]
        c = 6 - m
        re32[c // 2, at, (c % 2) * 128 : (c % 2) * 128 + 128] = high[PAD // 8 - m]


def kernel(
    rec, blk, qual, out,
    wh, v, mrg, rsb, piece, s, ab, re32, re, lhs, lext, own, snd, rcv,
    mrg_s, mrg_r, rs_s, rs_r, ag_s, ag_r, x_s, x_r, cx_s, cx_r, y_s, y_r,
):
    rx = lax.axis_index("rx")
    tm = lax.axis_index("tm")
    z, xh, c = rx // 4, (rx // 2) % 2, rx % 2
    y, xl = tm // 2, tm % 2

    def plane_peer(i):
        return (z + i // 4) % NZ, (xh + (i // 2) % 2) % 2, (xl + i % 2) % 2

    barrier = pltpu.get_barrier_semaphore()

    def greet(i, _):
        pz, pxh, pxl = plane_peer(i)
        pl.semaphore_signal(barrier, inc=1, device_id=device(pz, pxh, c, y, pxl), device_id_type=MESH)
        return 0

    lax.fori_loop(1, 4 * NZ, greet, 0)
    pl.semaphore_signal(barrier, inc=1, device_id=device(z, xh, 1 - c, y, xl), device_id_type=MESH)
    for g in range(1, NY):
        pl.semaphore_signal(barrier, inc=1, device_id=device(z, xh, c, (y + g) % NY, xl), device_id_type=MESH)

    ones = jnp.broadcast_to(qual[...].astype(F32), (128, 128))
    usable = jnp.transpose(ones)[:, :1]
    marks = []
    for k in range(2):
        b = blk[k]
        for half in range(2):
            marks.append((b == rx * 2 + half).astype(F32))
    for w in range(WIN):
        x = rec[:, w * W : (w + 1) * W]
        power = jnp.sum(x * x, axis=1, keepdims=True) * (1.0 / W)
        white = x * (lax.rsqrt(power + 1e-06) * usable)
        wh[:, w * W : (w + 1) * W] = white
        for t in range(2 * NY):
            rows = [
                white[8 * t : 8 * t + 8] * marks[2 * k] + white[64 + 8 * t : 72 + 8 * t] * marks[2 * k + 1]
                for k in range(2)
            ]
            v[t % 2, t // 2, :, w * W : (w + 1) * W] = jnp.concatenate(rows, 0).astype(BF16)

    pl.semaphore_wait(barrier, 4 * NZ - 1 + 1 + NY - 1)

    merge = pltpu.make_async_remote_copy(
        src_ref=v.at[:, pl.ds(2 * (1 - c), 2)], dst_ref=mrg, send_sem=mrg_s, recv_sem=mrg_r,
        device_id=device(z, xh, 1 - c, y, xl), device_id_type=MESH,
    )
    merge.start()

    def exchange(w):
        slot = ab.at[xl * WIN + w, pl.ds(PAD, W), pl.ds(0, 128)]
        return pltpu.make_async_remote_copy(
            src_ref=slot, dst_ref=slot, send_sem=x_s.at[w], recv_sem=x_r.at[w],
            device_id=device(z, xh, c, y, 1 - xl), device_id_type=MESH,
        )

    def scatter(i):
        pz, pxh = (z + i // 2) % NZ, (xh + i % 2) % 2
        return pltpu.make_async_remote_copy(
            src_ref=v.at[:, 2 * c + pxh, :, pl.ds(pl.multiple_of(pz * PIECE, 128), PIECE)],
            dst_ref=rsb.at[i], send_sem=rs_s.at[i], recv_sem=rs_r.at[i],
            device_id=device(pz, pxh, c, y, xl), device_id_type=MESH,
        )

    my_lanes = pl.ds(pl.multiple_of(xl * SHARE + z * PIECE, 128), PIECE)

    def gather(i):
        pz, pxh, pxl = plane_peer(i)
        return pltpu.make_async_remote_copy(
            src_ref=piece.at[pxl], dst_ref=s.at[2 * c + xh, :, my_lanes],
            send_sem=ag_s.at[i], recv_sem=ag_r.at[i],
            device_id=device(pz, pxh, c, y, pxl), device_id_type=MESH,
        )

    merge.wait()
    v[:, pl.ds(2 * c, 2)] = v[:, pl.ds(2 * c, 2)] + mrg[...]

    def run(fn):
        def step(i, _):
            fn(i)
            return 0
        return step

    lax.fori_loop(1, 2 * NZ, run(lambda i: scatter(i).start()), 0)

    zero_rows = jnp.zeros((PAD, 256), BF16)
    for w in range(2 * WIN):
        ab[w, 0:PAD, :] = zero_rows
        ab[w, PAD + W : ROWS, :] = zero_rows
    re32[...] = jnp.zeros_like(re32)
    for w in range(WIN):
        columns = jnp.transpose(wh[:, w * W : (w + 1) * W])
        at = xl * WIN + w
        ab[at, PAD : PAD + W, 0:128] = columns.astype(BF16)
        exchange(w).start()
        columns = columns.astype(BF16).astype(F32)
        fill_second_lane_half(ab, at, columns)
        fill_edges(re32, at, columns[:PAD], columns[W - PAD :])

    lax.fori_loop(1, 2 * NZ, run(lambda i: scatter(i).wait()), 0)
    total = v[:, 2 * c + xh, :, pl.ds(pl.multiple_of(z * PIECE, 128), PIECE)]
    total = lax.fori_loop(1, 2 * NZ, lambda i, t: t + rsb[i], total)
    piece[...] = total
    lax.fori_loop(1, 4 * NZ, run(lambda i: gather(i).start()), 0)
    s[2 * c + xh, :, my_lanes] = piece[xl]

    for w in range(WIN):
        at = (1 - xl) * WIN + w
        exchange(w).wait()
        columns = ab[at, PAD : PAD + W, 0:128].astype(F32)
        fill_second_lane_half(ab, at, columns)
        fill_edges(re32, at, columns[:PAD], columns[W - PAD :])
    re[...] = re32[...].astype(BF16)

    lax.fori_loop(1, 4 * NZ, run(lambda i: gather(i).wait()), 0)
    halves = s.at[pl.ds(2 * c, 2)]
    swap = pltpu.make_async_remote_copy(
        src_ref=halves, dst_ref=halves, send_sem=cx_s, recv_sem=cx_r,
        device_id=device(z, xh, 1 - c, y, xl), device_id_type=MESH,
    )
    swap.start()

    lane = lax.broadcasted_iota(jnp.int32, (16, 128), 1)

    def expand(group):
        top = pl.multiple_of(((group + NY - y) % NY) * 128, 128)

        def window(w, ext):
            x = s[group, :, pl.ds(pl.multiple_of(w * W, W), W)].astype(F32)
            results = []
            for f in range(FINE):
                shift = f - 2
                rows = pl.ds(pl.multiple_of(top + f * 16, 16), 16)
                moved = shifted_rows(x, shift)
                if shift > 0:
                    wraps, tile = lane < shift, 0
                else:
                    wraps, tile = lane >= 128 + shift, W - 128
                edge = moved[:, tile : tile + 128]
                kept = jnp.where(wraps, 0.0, edge)
                if tile == 0:
                    moved = jnp.concatenate([kept, moved[:, 128:]], 1)
                else:
                    moved = jnp.concatenate([moved[:, :tile], kept], 1)
                lhs[rows, pl.ds(pl.multiple_of(w * W, W), W)] = moved.astype(BF16)
                lost = jnp.where(wraps, edge, 0.0)
                results.append(ext[f] + pltpu.roll(lost, w * 8 + 2, 1))
            return tuple(results)

        ext = lax.fori_loop(0, 2 * WIN, window, tuple(jnp.zeros((16, 128), F32) for _ in range(FINE)))
        for f in range(FINE):
            rows = pl.ds(pl.multiple_of(top + f * 16, 16), 16)
            lext[rows, :] = ext[f].astype(BF16)

    lax.fori_loop(0, 2, run(lambda j: expand(2 * c + j)), 0)
    swap.wait()
    lax.fori_loop(0, 2, run(lambda j: expand(2 * (1 - c) + j)), 0)

    def reduce_copy(g, p, lanes=256):
        return pltpu.make_async_remote_copy(
            src_ref=snd.at[g - 1, p, :, pl.ds(0, lanes)], dst_ref=rcv.at[g - 1, p, :, pl.ds(0, lanes)],
            send_sem=y_s.at[g - 1, p], recv_sem=y_r.at[g - 1, p],
            device_id=device(z, xh, c, (y + g) % NY, xl), device_id_type=MESH,
        )

    def correlate(p, lanes=256):
        acc = jnp.dot(lext[...], re[p, :, :lanes], preferred_element_type=F32)
        for w in range(2 * WIN):
            acc += jnp.dot(
                lhs[:, w * W : (w + 1) * W],
                ab[w, pl.ds(pl.multiple_of(p * 16, 16), W), 0:lanes],
                preferred_element_type=F32,
            )
        own[p, :, :lanes] = acc[:128]
        for g in range(1, NY):
            snd[g - 1, p, :, :lanes] = acc[128 * g : 128 * g + 128].astype(BF16)
            reduce_copy(g, p, lanes).start()

    lax.fori_loop(0, PAIRS - 1, run(correlate), 0)
    correlate(PAIRS - 1, 128)

    def finish(p, lanes=256):
        for g in range(1, NY):
            reduce_copy(g, p, lanes).wait()
        acc = own[p, :, :lanes]
        for g in range(1, NY):
            acc += rcv[g - 1, p, :, :lanes].astype(F32)
        acc *= WEIGHT
        for h in range(lanes // 128):
            out[2 * p + h] = acc[:, 128 * h : 128 * h + 128]

    lax.fori_loop(0, PAIRS - 1, run(finish), 0)
    finish(PAIRS - 1, 128)


def on_device(records, source_block, quality):
    vmem = pl.BlockSpec(memory_space=pltpu.VMEM)
    dma = pltpu.SemaphoreType.DMA
    sums = pl.pallas_call(
        kernel,
        out_shape=jax.ShapeDtypeStruct((COARSE, 128, 128), F32),
        in_specs=[vmem, pl.BlockSpec(memory_space=pltpu.SMEM), vmem],
        out_specs=vmem,
        scratch_shapes=[
            pltpu.VMEM((128, SHARE), F32),
            pltpu.VMEM((2, NY, 16, SHARE), BF16),
            pltpu.VMEM((2, 2, 16, SHARE), BF16),
            pltpu.VMEM((2 * NZ, 2, 16, PIECE), BF16),
            pltpu.VMEM((2, 16, PIECE), BF16),
            pltpu.VMEM((NY, 16, 2 * SHARE), BF16),
            pltpu.VMEM((2 * WIN, ROWS, 256), BF16),
            pltpu.VMEM((PAIRS, 128, 256), F32),
            pltpu.VMEM((PAIRS, 128, 256), BF16),
            pltpu.VMEM((NY * 128, 2 * SHARE), BF16),
            pltpu.VMEM((NY * 128, 128), BF16),
            pltpu.VMEM((PAIRS, 128, 256), F32),
            pltpu.VMEM((NY - 1, PAIRS, 128, 256), BF16),
            pltpu.VMEM((NY - 1, PAIRS, 128, 256), BF16),
            dma, dma, dma((2 * NZ,)), dma((2 * NZ,)), dma((4 * NZ,)), dma((4 * NZ,)),
            dma((WIN,)), dma((WIN,)), dma, dma, dma((NY - 1, PAIRS)), dma((NY - 1, PAIRS)),
        ],
        compiler_params=pltpu.CompilerParams(
            collective_id=0, has_side_effects=True, vmem_limit_bytes=56 << 20
        ),
        name="correlate",
    )(records, source_block, quality.reshape(1, 128))
    stacks = sums.reshape(COARSE, FINE, 2, 8, 128).transpose(2, 3, 0, 1, 4)
    return stacks.reshape(2, 8, COARSE * FINE, 128)[:, :, :LAGS]


def solution(mesh):
    in_specs = (P("rx", "tm"), P(), P("rx"))
    out_specs = P(None, "tm", None, "rx")
    return jax.shard_map(
        on_device, mesh=mesh, in_specs=in_specs, out_specs=out_specs, check_vma=False
    )
```

time: 486 us -> 73.8 us (0.15)
  waiting for transfers between devices: 408 us -> 0 us
  Pallas kernels: 0 us -> 71.4 us
  local copies, waits for them, and re-layouts: 31.1 us -> 2.2 us
  matrix products: 22.9 us -> 0 us
  between operations: 14.5 us -> 0.02 us
  other arithmetic: 8.97 us -> 0 us
    psum x1 -> x0, waiting for transfers between devices: 266 us -> none  [broadcast(): return lax.psum(block, axis)]
    reduce_scatter x2 -> x0, waiting for transfers between devices: 142 us -> none  [on_device(): lax.psum_scatter(step_term(jnp.int32(0), share_rows * lax.axis_size('tm')...]
    pallas_call x0 -> x1, Pallas kernels: none -> 71.4 us  [on_device(): pl.pallas_call(kernel, out_shape=jax.ShapeDtypeStruct((COARSE, 128, 128),...]
    unnamed x36 -> x0, local copies, waits for them, and re-layouts: 27.6 us -> none
    dot_general x2 -> x0, matrix products: 22.9 us -> none  [lag_products(): lax.dot_general(source_rows, receiver_rows, (((1,), (1,)), ((), ())), pre...]
  transfers between devices with their start and end apart: 3 -> 0, of which waited for: 3 -> 0; matrix products, arithmetic and copies ran while one was open for 5% -> 0% of each run, Pallas kernels for 0% -> 0%
where the time goes in v1:
time: 73.8 us; the launch traced here: 73.6 us
  Pallas kernels  71.4 us (97%)
  local copies, waits for them, and re-layouts  2.2 us (3%)
    pallas_call x1, Pallas kernels, on_device(): pl.pallas_call(kernel, out_shape=jax.ShapeDtypeStruct((COARSE, 128, 128),...  71.4 us

profile of v1, /device:TPU:1, one launch (start us, length us, event | category | flops | bytes accessed | tf_op | source)
XLA Modules:
  0.0 73.6 jit_solution(3684870327832146393)
XLA Ops:
  0.0 71.4 %correlate.1 = f32[13,128,128]{2,1,0:T(8,128)} custom-call(f32[128,3072]{1,0:T(8,128)} %rec.1, s32[2]{0:T(128)} %blk.1, s32[1,128]{1,0:T(1,128)} %bitcast.7), custom_call_target="tpu_custom_call" | custom-call | tf_op jit(solution)/shard_map/correlate/pallas_call | solution.py:261
  71.4 1.2 %copy.4 = f32[2,8,13,8,128]{4,1,3,2,0:T(8,128)S(1)} copy(f32[2,8,13,8,128]{4,1,0,3,2:T(8,128)} %bitcast.5) | data formatting | bytes 1703936 | tf_op jit(solution)/shard_map/transpose | solution.py:289
  72.7 1.0 %slice.4 = f32[2,8,101,128]{3,1,2,0:T(8,128)} slice(f32[2,8,104,128]{3,1,2,0:T(8,128)S(1)} %bitcast.6), slice={[0:2], [0:8], [0:101], [0:128]} | slice | bytes 1654784 | tf_op jit(solution)/shard_map/slice | solution.py:290

commit v2 on v1

v2 whole, which is shorter than its diff:
```python
import math

import jax
import jax.numpy as jnp
from jax import lax
from jax.experimental import pallas as pl
from jax.experimental.pallas import tpu as pltpu
from jax.sharding import PartitionSpec as P

W = 1024
LAGS = 101
FINE = 8
COARSE = 13
PAD = 48
NZ = 8
NY = 4
WIN = 3
ROWS = W + 2 * PAD
SHARE = WIN * W
PIECE = SHARE // NZ
PAIRS = (COARSE + 1) // 2
WEIGHT = 1.0 / math.sqrt(24 * W)
MESH = pl.DeviceIdType.MESH
F32 = jnp.float32
BF16 = jnp.bfloat16


def device(z, xh, c, y, xl):
    return ((z * 2 + xh) * 2 + c, y * 2 + xl)


def shifted_rows(values, shift):
    return pltpu.roll(values, shift % values.shape[1], 1)


def fill_second_lane_half(ab, w, columns):
    zeros = jnp.zeros((8, 128), F32)
    ab[w, PAD - 16 : PAD + W, 128:256] = jnp.concatenate([zeros, columns, zeros], 0).astype(BF16)


def edge_rows(block, keep_low):
    blocks = block.reshape(PAD // 8, 8, 128)
    rolled = pltpu.roll(blocks, 2, 1)
    row = lax.broadcasted_iota(jnp.int32, rolled.shape, 1)
    keep = row < 2 if keep_low else row >= 2
    return jnp.where(keep, rolled, 0.0)


def fill_edges(re32, w, head, tail):
    low = edge_rows(head, True)
    high = edge_rows(tail, False)
    at = pl.ds(pl.multiple_of(w * 8, 8), 8)
    for m in range(1, PAD // 8 + 1):
        c = 6 + m
        re32[c // 2, at, (c % 2) * 128 : (c % 2) * 128 + 128] = low[m - 1]
        c = 6 - m
        re32[c // 2, at, (c % 2) * 128 : (c % 2) * 128 + 128] = high[PAD // 8 - m]


def kernel(
    rec, blk, qual, out,
    wh, v, mrg, rsb, piece, s, ab, re32, re, lhs, lext, own, ysnd, yrcv, xsnd, xrcv,
    mrg_s, mrg_r, rs_s, rs_r, ag_s, ag_r, ex_s, ex_r, cx_s, cx_r, y_s, y_r, x_s, x_r, ready,
):
    rx = lax.axis_index("rx")
    tm = lax.axis_index("tm")
    z, xh, c = rx // 4, (rx // 2) % 2, rx % 2
    y, xl = tm // 2, tm % 2
    sibling = device(z, xh, 1 - c, y, xl)

    def plane_peer(i):
        return (z + i // 2) % NZ, (xh + i % 2) % 2

    def run(fn):
        def step(i, _):
            fn(i)
            return 0

        return step

    barrier = pltpu.get_barrier_semaphore()

    def greet(peer):
        pl.semaphore_signal(barrier, inc=1, device_id=peer, device_id_type=MESH)

    greet(sibling)
    lax.fori_loop(1, 2 * NZ, run(lambda i: greet(device(*plane_peer(i), c, y, xl))), 0)
    for g in range(1, NY):
        greet(device(z, xh, c, (y + g) % NY, xl))
    greet(device(z, xh, c, y, 1 - xl))

    ones = jnp.broadcast_to(qual[...].astype(F32), (128, 128))
    usable = jnp.transpose(ones)[:, :1]
    marks = []
    for k in range(2):
        b = blk[k]
        for half in range(2):
            marks.append((b == rx * 2 + half).astype(F32))
    for w in range(WIN):
        x = rec[:, w * W : (w + 1) * W]
        power = jnp.sum(x * x, axis=1, keepdims=True) * (1.0 / W)
        white = x * (lax.rsqrt(power + 1e-06) * usable)
        wh[:, w * W : (w + 1) * W] = white
        for k in range(2):
            rows = white[:64] * marks[2 * k] + white[64:] * marks[2 * k + 1]
            v[k, :, :, w * W : (w + 1) * W] = rows.astype(BF16).reshape(NY, 16, W)

    zero_rows = jnp.zeros((PAD, 256), BF16)
    for w in range(2 * WIN):
        ab[w, 0:PAD, :] = zero_rows
        ab[w, PAD + W : ROWS, :] = zero_rows
    re32[...] = jnp.zeros_like(re32)
    for w in range(WIN):
        columns = jnp.transpose(wh[:, w * W : (w + 1) * W]).astype(BF16)
        at = (y // 2) * WIN + w
        ab[at, PAD : PAD + W, 0:128] = columns
        columns = columns.astype(F32)
        fill_second_lane_half(ab, at, columns)
        fill_edges(re32, at, columns[:PAD], columns[W - PAD :])

    pl.semaphore_wait(barrier, 1 + (2 * NZ - 1) + NY)
    pl.semaphore_signal(ready, inc=1, device_id=device(z, xh, c, (y + 2) % NY, xl), device_id_type=MESH)

    def merge(j):
        yd = (y + 1 + 2 * j + j // 2) % NY
        return pltpu.make_async_remote_copy(
            src_ref=v.at[1 - c, yd], dst_ref=mrg.at[yd], send_sem=mrg_s.at[j], recv_sem=mrg_r.at[j],
            device_id=sibling, device_id_type=MESH,
        )

    def exchange(w):
        slot = ab.at[(y // 2) * WIN + w, pl.ds(PAD, W), pl.ds(0, 128)]
        return pltpu.make_async_remote_copy(
            src_ref=slot, dst_ref=slot, send_sem=ex_s.at[w], recv_sem=ex_r.at[w],
            device_id=device(z, xh, c, (y + 2) % NY, xl), device_id_type=MESH,
        )

    def group_of(h, xd):
        if h == 0:
            return (y + 3 + 2 * ((c + xd) % 2)) % NY
        return (y + 2 * xd) % NY

    def scatter(h, i):
        pz, pxh = plane_peer(i)
        return pltpu.make_async_remote_copy(
            src_ref=v.at[c, group_of(h, pxh), :, pl.ds(pl.multiple_of(pz * PIECE, 128), PIECE)],
            dst_ref=rsb.at[h, i], send_sem=rs_s.at[h, i], recv_sem=rs_r.at[h, i],
            device_id=device(pz, pxh, c, y, xl), device_id_type=MESH,
        )

    my_lanes = pl.ds(pl.multiple_of((y // 2) * SHARE + z * PIECE, 128), PIECE)

    def gather(h, i):
        return pltpu.make_async_remote_copy(
            src_ref=piece.at[h], dst_ref=s.at[h, c, :, my_lanes],
            send_sem=ag_s.at[h, i], recv_sem=ag_r.at[h, i],
            device_id=device(*plane_peer(i), c, (y + 2 * xh) % NY, xl), device_id_type=MESH,
        )

    def swap(h):
        return pltpu.make_async_remote_copy(
            src_ref=s.at[h, c], dst_ref=s.at[h, c], send_sem=cx_s.at[h], recv_sem=cx_r.at[h],
            device_id=sibling, device_id_type=MESH,
        )

    for j in range(NY):
        merge(j).start()
    for w in range(WIN):
        exchange(w).start()
    def scatter_half(h):
        for j in range(2):
            merge(2 * h + j).wait_recv()
            yd = (y + 1 + 2 * j + h) % NY
            v[c, yd] = v[c, yd] + mrg[yd]
        for i in range(1, 2 * NZ):
            scatter(h, i).start()

    def gather_half(h):
        total = v[c, group_of(h, xh), :, pl.ds(pl.multiple_of(z * PIECE, 128), PIECE)]
        for i in range(1, 2 * NZ):
            scatter(h, i).wait_recv()
            total += rsb[h, i]
        piece[h] = total

        @pl.when(xh == 1)
        def _():
            gather(h, 0).start()

        for i in range(1, 2 * NZ):
            gather(h, i).start()

        @pl.when(xh == 0)
        def _():
            s[h, c, :, my_lanes] = piece[h]

    scatter_half(0)
    pl.semaphore_wait(ready, 1)
    gather_half(0)
    scatter_half(1)

    for w in range(WIN):
        at = (1 - y // 2) * WIN + w
        exchange(w).wait_recv()
        columns = ab[at, PAD : PAD + W, 0:128].astype(F32)
        fill_second_lane_half(ab, at, columns)
        fill_edges(re32, at, columns[:PAD], columns[W - PAD :])
    re[...] = re32[...].astype(BF16)

    def gathered(h):
        @pl.when(xh == 1)
        def _():
            gather(h, 0).wait_recv()

        for i in range(1, 2 * NZ):
            gather(h, i).wait_recv()

    def sent(h):
        @pl.when(xh == 1)
        def _():
            gather(h, 0).wait_send()

        lax.fori_loop(1, 2 * NZ, run(lambda i: gather(h, i).wait_send()), 0)
        lax.fori_loop(1, 2 * NZ, run(lambda i: scatter(h, i).wait_send()), 0)
        for j in range(2):
            merge(2 * h + j).wait_send()
        swap(h).wait_send()

    lane = lax.broadcasted_iota(jnp.int32, (16, 128), 1)

    def expand(h, k):
        def window(w, ext):
            at = pl.ds(pl.multiple_of(w * W, W), W)
            x = s[h, k, :, at].astype(F32)
            results = []
            for f in range(FINE):
                shift = f - 2
                rows = pl.ds(pl.multiple_of(k * 128 + f * 16, 16), 16)
                moved = shifted_rows(x, shift)
                if shift > 0:
                    wraps, tile = lane < shift, 0
                else:
                    wraps, tile = lane >= 128 + shift, W - 128
                edge = moved[:, tile : tile + 128]
                kept = jnp.where(wraps, 0.0, edge)
                if tile == 0:
                    moved = jnp.concatenate([kept, moved[:, 128:]], 1)
                else:
                    moved = jnp.concatenate([moved[:, :tile], kept], 1)
                lhs[h, rows, at] = moved.astype(BF16)
                lost = jnp.where(wraps, edge, 0.0)
                results.append(ext[f] + pltpu.roll(lost, w * 8 + 2, 1))
            return tuple(results)

        ext = lax.fori_loop(0, 2 * WIN, window, tuple(jnp.zeros((16, 128), F32) for _ in range(FINE)))
        for f in range(FINE):
            lext[h, pl.ds(pl.multiple_of(k * 128 + f * 16, 16), 16), :] = ext[f].astype(BF16)

    def correlate(h, p, lanes):
        acc = jnp.dot(lext[h], re[p, :, :lanes], preferred_element_type=F32)
        for w in range(2 * WIN):
            acc += jnp.dot(
                lhs[h, :, w * W : (w + 1) * W],
                ab[w, pl.ds(pl.multiple_of(p * 16, 16), W), 0:lanes],
                preferred_element_type=F32,
            )
        return acc

    def y_copy(k, p, lanes):
        return pltpu.make_async_remote_copy(
            src_ref=ysnd.at[k, p, :, pl.ds(0, lanes)], dst_ref=yrcv.at[k, p, :, pl.ds(0, lanes)],
            send_sem=y_s.at[k, p], recv_sem=y_r.at[k, p],
            device_id=device(z, xh, c, (y + 3 + 2 * k) % NY, xl), device_id_type=MESH,
        )

    def x_copy(p, lanes):
        return pltpu.make_async_remote_copy(
            src_ref=xsnd.at[p, :, pl.ds(0, lanes)], dst_ref=xrcv.at[p, :, pl.ds(0, lanes)],
            send_sem=x_s.at[p], recv_sem=x_r.at[p],
            device_id=device(z, xh, c, y, 1 - xl), device_id_type=MESH,
        )

    def first(p, lanes=256):
        acc = correlate(0, p, lanes)
        for k in range(2):
            ysnd[k, p, :, :lanes] = acc[128 * k : 128 * k + 128].astype(BF16)
            y_copy(k, p, lanes).start()

    def second(p, lanes=256):
        acc = correlate(1, p, lanes)
        mine, other = [], []
        for k in range(2):
            y_copy(k, p, lanes).wait_recv()
            both = acc[128 * k : 128 * k + 128] + yrcv[k, p, :, :lanes].astype(F32)
            both = both.reshape(FINE, 2, 8, lanes)
            low, high = both[:, 0].reshape(64, lanes), both[:, 1].reshape(64, lanes)
            mine.append(jnp.where(xl == 0, low, high))
            other.append(jnp.where(xl == 0, high, low))
        own[p, :, :lanes] = jnp.concatenate(mine, 0)
        xsnd[p, :, :lanes] = jnp.concatenate(other, 0).astype(BF16)
        x_copy(p, lanes).start()

    def finish(p, lanes=256):
        x_copy(p, lanes).wait_recv()
        acc = (own[p, :, :lanes] + xrcv[p, :, :lanes].astype(F32)) * WEIGHT
        for g in range(lanes // 128):
            out[2 * p + g] = acc[:, 128 * g : 128 * g + 128]

    gathered(0)
    swap(0).start()
    gather_half(1)
    expand(0, c)
    swap(0).wait_recv()
    expand(0, 1 - c)
    lax.fori_loop(0, PAIRS - 1, run(first), 0)
    gathered(1)
    swap(1).start()
    first(PAIRS - 1, 128)
    expand(1, c)
    swap(1).wait_recv()
    expand(1, 1 - c)
    lax.fori_loop(0, PAIRS - 1, run(second), 0)
    second(PAIRS - 1, 128)

    for h in range(2):
        sent(h)
    for w in range(WIN):
        exchange(w).wait_send()

    def all_sent(p, lanes=256):
        for k in range(2):
            y_copy(k, p, lanes).wait_send()
        x_copy(p, lanes).wait_send()

    lax.fori_loop(0, PAIRS - 1, run(all_sent), 0)
    all_sent(PAIRS - 1, 128)
    lax.fori_loop(0, PAIRS - 1, run(finish), 0)
    finish(PAIRS - 1, 128)


def on_device(records, source_block, quality):
    vmem = pl.BlockSpec(memory_space=pltpu.VMEM)
    dma = pltpu.SemaphoreType.DMA
    sums = pl.pallas_call(
        kernel,
        out_shape=jax.ShapeDtypeStruct((COARSE, 128, 128), F32),
        in_specs=[vmem, pl.BlockSpec(memory_space=pltpu.SMEM), vmem],
        out_specs=vmem,
        scratch_shapes=[
            pltpu.VMEM((128, SHARE), F32),
            pltpu.VMEM((2, NY, 16, SHARE), BF16),
            pltpu.VMEM((NY, 16, SHARE), BF16),
            pltpu.VMEM((2, 2 * NZ, 16, PIECE), BF16),
            pltpu.VMEM((2, 16, PIECE), BF16),
            pltpu.VMEM((2, 2, 16, 2 * SHARE), BF16),
            pltpu.VMEM((2 * WIN, ROWS, 256), BF16),
            pltpu.VMEM((PAIRS, 128, 256), F32),
            pltpu.VMEM((PAIRS, 128, 256), BF16),
            pltpu.VMEM((2, 256, 2 * SHARE), BF16),
            pltpu.VMEM((2, 256, 128), BF16),
            pltpu.VMEM((PAIRS, 128, 256), F32),
            pltpu.VMEM((2, PAIRS, 128, 256), BF16),
            pltpu.VMEM((2, PAIRS, 128, 256), BF16),
            pltpu.VMEM((PAIRS, 128, 256), BF16),
            pltpu.VMEM((PAIRS, 128, 256), BF16),
            dma((NY,)), dma((NY,)), dma((2, 2 * NZ)), dma((2, 2 * NZ)), dma((2, 2 * NZ)), dma((2, 2 * NZ)),
            dma((WIN,)), dma((WIN,)), dma((2,)), dma((2,)),
            dma((2, PAIRS)), dma((2, PAIRS)), dma((PAIRS,)), dma((PAIRS,)),
            pltpu.SemaphoreType.REGULAR,
        ],
        compiler_params=pltpu.CompilerParams(
            collective_id=0, has_side_effects=True, vmem_limit_bytes=56 << 20
        ),
        name="correlate",
    )(records, source_block, quality.reshape(1, 128))
    stacks = sums.reshape(COARSE, 2, FINE, 8, 128).transpose(1, 3, 0, 2, 4)
    return stacks.reshape(2, 8, COARSE * FINE, 128)[:, :, :LAGS]


def solution(mesh):
    in_specs = (P("rx", "tm"), P(), P("rx"))
    out_specs = P(None, "tm", None, "rx")
    return jax.shard_map(
        on_device, mesh=mesh, in_specs=in_specs, out_specs=out_specs, check_vma=False
    )
```

time: 73.8 us -> 63.2 us (0.86)
  Pallas kernels: 71.4 us -> 60.9 us
    pallas_call x1, Pallas kernels: 71.4 us -> 60.9 us  [on_device(): pl.pallas_call(kernel, out_shape=jax.ShapeDtypeStruct((COARSE, 128, 128),...]
where the time goes in v2:
time: 63.2 us; the launch traced here: 63.1 us
  Pallas kernels  60.9 us (96%)
  local copies, waits for them, and re-layouts  2.18 us (3%)
    pallas_call x1, Pallas kernels, on_device(): pl.pallas_call(kernel, out_shape=jax.ShapeDtypeStruct((COARSE, 128, 128),...  60.9 us

profile of v2, /device:TPU:1, one launch (start us, length us, event | category | flops | bytes accessed | tf_op | source)
XLA Modules:
  0.0 63.1 jit_solution(15357632894768689857)
XLA Ops:
  0.0 60.9 %correlate.1 = f32[13,128,128]{2,1,0:T(8,128)} custom-call(f32[128,3072]{1,0:T(8,128)} %rec.1, s32[2]{0:T(128)} %blk.1, s32[1,128]{1,0:T(1,128)} %bitcast.7), custom_call_target="tpu_custom_call" | custom-call | tf_op jit(solution)/shard_map/correlate/pallas_call | solution.py:343
  60.9 1.2 %copy.4 = f32[2,8,13,8,128]{4,1,3,2,0:T(8,128)S(1)} copy(f32[2,8,13,8,128]{4,1,3,0,2:T(8,128)} %bitcast.5) | data formatting | bytes 1703936 | tf_op jit(solution)/shard_map/transpose | solution.py:375
  62.1 1.0 %slice.4 = f32[2,8,101,128]{3,1,2,0:T(8,128)} slice(f32[2,8,104,128]{3,1,2,0:T(8,128)S(1)} %bitcast.6), slice={[0:2], [0:8], [0:101], [0:128]} | slice | bytes 1654784 | tf_op jit(solution)/shard_map/slice | solution.py:376

commit v3 on v2

--- a/solution.py
+++ b/solution.py
@@ -58,9 +58,9 @@
 
 
 def kernel(
-    rec, blk, qual, out,
-    wh, v, mrg, rsb, piece, s, ab, re32, re, lhs, lext, own, ysnd, yrcv, xsnd, xrcv,
-    mrg_s, mrg_r, rs_s, rs_r, ag_s, ag_r, ex_s, ex_r, cx_s, cx_r, y_s, y_r, x_s, x_r, ready,
+    rec_hbm, blk, qual, out,
+    rec,     wh, v, mrg, rsb, piece, s, ab, re32, re, lhs, lext, own, ysnd, yrcv, xsnd, xrcv,
+    mrg_s, mrg_r, rs_s, rs_r, ag_s, ag_r, ex_s, ex_r, cx_s, cx_r, y_s, y_r, x_s, x_r, ready, rec_sem,
 ):
     rx = lax.axis_index("rx")
     tm = lax.axis_index("tm")
@@ -88,6 +88,13 @@
     for g in range(1, NY):
         greet(device(z, xh, c, (y + g) % NY, xl))
     greet(device(z, xh, c, y, 1 - xl))
+
+    def load(w):
+        at = pl.ds(w * W, W)
+        return pltpu.make_async_copy(rec_hbm.at[:, at], rec.at[:, at], rec_sem.at[w])
+
+    for w in range(WIN):
+        load(w).start()
 
     ones = jnp.broadcast_to(qual[...].astype(F32), (128, 128))
     usable = jnp.transpose(ones)[:, :1]
@@ -97,6 +104,7 @@
         for half in range(2):
             marks.append((b == rx * 2 + half).astype(F32))
     for w in range(WIN):
+        load(w).wait()
         x = rec[:, w * W : (w + 1) * W]
         power = jnp.sum(x * x, axis=1, keepdims=True) * (1.0 / W)
         white = x * (lax.rsqrt(power + 1e-06) * usable)
@@ -343,9 +351,10 @@
     sums = pl.pallas_call(
         kernel,
         out_shape=jax.ShapeDtypeStruct((COARSE, 128, 128), F32),
-        in_specs=[vmem, pl.BlockSpec(memory_space=pltpu.SMEM), vmem],
+        in_specs=[pl.BlockSpec(memory_space=pl.ANY), pl.BlockSpec(memory_space=pltpu.SMEM), vmem],
         out_specs=vmem,
         scratch_shapes=[
+            pltpu.VMEM((128, SHARE), F32),
             pltpu.VMEM((128, SHARE), F32),
             pltpu.VMEM((2, NY, 16, SHARE), BF16),
             pltpu.VMEM((NY, 16, SHARE), BF16),
@@ -365,7 +374,7 @@
             dma((NY,)), dma((NY,)), dma((2, 2 * NZ)), dma((2, 2 * NZ)), dma((2, 2 * NZ)), dma((2, 2 * NZ)),
             dma((WIN,)), dma((WIN,)), dma((2,)), dma((2,)),
             dma((2, PAIRS)), dma((2, PAIRS)), dma((PAIRS,)), dma((PAIRS,)),
-            pltpu.SemaphoreType.REGULAR,
+            pltpu.SemaphoreType.REGULAR, dma((WIN,)),
         ],
         compiler_params=pltpu.CompilerParams(
             collective_id=0, has_side_effects=True, vmem_limit_bytes=56 << 20

time: 63.2 us -> 62.3 us (0.986)
  Pallas kernels: 60.9 us -> 60 us
    pallas_call x1, Pallas kernels: 60.9 us -> 60 us  [on_device(): pl.pallas_call(kernel, out_shape=jax.ShapeDtypeStruct((COARSE, 128, 128),...]
where the time goes in v3:
time: 62.3 us; the launch traced here: 62.2 us
  Pallas kernels  60 us (96%)
  local copies, waits for them, and re-layouts  2.18 us (3%)
    pallas_call x1, Pallas kernels, on_device(): pl.pallas_call(kernel, out_shape=jax.ShapeDtypeStruct((COARSE, 128, 128),...  60 us

profile of v3, /device:TPU:1, one launch (start us, length us, event | category | flops | bytes accessed | tf_op | source)
XLA Modules:
  0.0 62.2 jit_solution(684813479382192837)
XLA Ops:
  0.0 60.0 %correlate.1 = f32[13,128,128]{2,1,0:T(8,128)} custom-call(f32[128,3072]{1,0:T(8,128)} %rec_hbm.1, s32[2]{0:T(128)} %blk.1, s32[1,128]{1,0:T(1,128)} %bitcast.7), custom_call_target="tpu_custom_call" | custom-call | tf_op jit(solution)/shard_map/correlate/pallas_call | solution.py:351
  60.0 1.2 %copy.4 = f32[2,8,13,8,128]{4,1,3,2,0:T(8,128)S(1)} copy(f32[2,8,13,8,128]{4,1,3,0,2:T(8,128)} %bitcast.5) | data formatting | bytes 1703936 | tf_op jit(solution)/shard_map/transpose | solution.py:384
  61.2 1.0 %slice.4 = f32[2,8,101,128]{3,1,2,0:T(8,128)} slice(f32[2,8,104,128]{3,1,2,0:T(8,128)S(1)} %bitcast.6), slice={[0:2], [0:8], [0:101], [0:128]} | slice | bytes 1654784 | tf_op jit(solution)/shard_map/slice | solution.py:385

commit v4 on v3

--- a/solution.py
+++ b/solution.py
@@ -315,8 +315,8 @@
 
     gathered(0)
     swap(0).start()
+    expand(0, c)
     gather_half(1)
-    expand(0, c)
     swap(0).wait_recv()
     expand(0, 1 - c)
     lax.fori_loop(0, PAIRS - 1, run(first), 0)
@@ -329,6 +329,9 @@
     lax.fori_loop(0, PAIRS - 1, run(second), 0)
     second(PAIRS - 1, 128)
 
+    lax.fori_loop(0, PAIRS - 1, run(finish), 0)
+    finish(PAIRS - 1, 128)
+
     for h in range(2):
         sent(h)
     for w in range(WIN):
@@ -341,8 +344,6 @@
 
     lax.fori_loop(0, PAIRS - 1, run(all_sent), 0)
     all_sent(PAIRS - 1, 128)
-    lax.fori_loop(0, PAIRS - 1, run(finish), 0)
-    finish(PAIRS - 1, 128)
 
 
 def on_device(records, source_block, quality):

time: 62.3 us -> 62.8 us (level)
  no operation moved by 1% of the time
where the time goes in v4:
time: 62.8 us; the launch traced here: 62.6 us
  Pallas kernels  60.4 us (96%)
  local copies, waits for them, and re-layouts  2.18 us (3%)
    pallas_call x1, Pallas kernels, on_device(): pl.pallas_call(kernel, out_shape=jax.ShapeDtypeStruct((COARSE, 128, 128),...  60.4 us

profile of v4, /device:TPU:1, one launch (start us, length us, event | category | flops | bytes accessed | tf_op | source)
XLA Modules:
  0.0 62.6 jit_solution(11908087588798312569)
XLA Ops:
  0.0 60.4 %correlate.1 = f32[13,128,128]{2,1,0:T(8,128)} custom-call(f32[128,3072]{1,0:T(8,128)} %rec_hbm.1, s32[2]{0:T(128)} %blk.1, s32[1,128]{1,0:T(1,128)} %bitcast.7), custom_call_target="tpu_custom_call" | custom-call | tf_op jit(solution)/shard_map/correlate/pallas_call | solution.py:352
  60.4 1.2 %copy.4 = f32[2,8,13,8,128]{4,1,3,2,0:T(8,128)S(1)} copy(f32[2,8,13,8,128]{4,1,3,0,2:T(8,128)} %bitcast.5) | data formatting | bytes 1703936 | tf_op jit(solution)/shard_map/transpose | solution.py:385
  61.7 1.0 %slice.4 = f32[2,8,101,128]{3,1,2,0:T(8,128)} slice(f32[2,8,104,128]{3,1,2,0:T(8,128)S(1)} %bitcast.6), slice={[0:2], [0:8], [0:101], [0:128]} | slice | bytes 1654784 | tf_op jit(solution)/shard_map/slice | solution.py:386
